TPU v7x, 32 devices: a whole 2x2x4 slice. The times are simulated.
32 devices in a mesh: groups: 2 (over y), tok: 16 (over z, x, core).
Axes of the slice: x: 2, y: 2, z: 4, core: 2. Of those that a mesh axis runs over, the one named last changes fastest.
Arguments:
- activations: bfloat16 [2, 20480, 2048], P(None, ('groups', 'tok')), parts along dimension 1, may hold values from -6 to 6
- gradients: bfloat16 [2, 20480, 2048], P(None, ('groups', 'tok')), parts along dimension 1, may hold values from -6 to 6
- query_u: bfloat16 [4, 2048, 1024], P('groups', 'tok'), parts along dimension 0, may hold values from -4 to 4
- query_v: bfloat16 [4, 2048, 1024], P('groups', 'tok'), parts along dimension 0, may hold values from -4 to 4
- block_ids: int32 [4, 16], P('groups'), parts along dimension 0, may hold values from 0 to 31
- counts: int32 [32], P(('groups', 'tok')), parts along dimension 0, may hold values from 1 to 640, 5440 in all
Outputs:
- scores: float32 [20480, 64], P(('groups', 'tok')), parts along dimension 0
There are 2 independent parts, one for each index of `groups`. A program takes and returns all parts, laid end to end along the dimension named above; each array names one. Nothing has to cross between parts.
Inputs may be any that keep to these rules, and one draw needn't show every extreme that they name: The counts of one part sum to (16 + 1) * 320 and the largest equals 640.
All inputs are finite; a program needn't handle non-finite values. No bound on the sum of `counts` on one device may be relied on, other than what follows from the above.
Results may differ from a plain program's by a relative error of at most 0.0003.
Values may be sent and summed in bfloat16 or wider, within the bound.
A program may use at most 64 MiB of HBM per device.

v0:
```python
import jax
import jax.numpy as jnp
from jax import lax
from jax.sharding import PartitionSpec as P

RANK = 8
QB = 4


def pick_columns(factor, block_ids):
    width = QB * RANK
    chosen = []
    for layer in range(factor.shape[0]):
        slots = factor[layer].reshape(factor.shape[1], -1, width)
        chosen.append(jnp.take(slots, block_ids[layer], axis=1).reshape(factor.shape[1], -1))
    return jnp.stack(chosen)


def rank_grams(factor):
    per = factor.reshape(factor.shape[0], factor.shape[1], -1, RANK)
    return jnp.einsum("lkqr,lkqs->lqrs", per, per, preferred_element_type=jnp.float32)


def per_device(activations, gradients, query_u, query_v, block_ids, counts):
    layers, tok_rows, width = activations.shape
    columns = block_ids.shape[1] * QB * RANK
    queries = columns // RANK
    picked_u = pick_columns(query_u, block_ids)
    picked_v = pick_columns(query_v, block_ids)
    whole_u, whole_v = (
        lax.all_gather(picked_u, "tok", axis=1, tiled=True),
        lax.all_gather(picked_v, "tok", axis=1, tiled=True),
    )
    grad_proj = jnp.einsum("ltk,lkc->ltc", gradients, whole_u, preferred_element_type=jnp.float32)
    act_proj = jnp.einsum("ltk,lkc->ltc", activations, whole_v, preferred_element_type=jnp.float32)
    totals = (grad_proj, act_proj)
    totals = totals + (rank_grams(whole_u), rank_grams(whole_v))
    gram_u = totals[2]
    gram_v = totals[3]
    raw = jnp.sum((totals[0] * totals[1]).reshape(layers, tok_rows, queries, RANK), axis=(0, 3))
    norm_sq = jnp.sum(gram_u * gram_v, axis=(0, 2, 3))
    live = jnp.arange(tok_rows, dtype=jnp.int32) < counts[0]
    scaled = raw / jnp.sqrt(norm_sq + 1e-06)[None, :]
    return jnp.where(live[:, None], scaled, jnp.zeros_like(scaled))


def solution(mesh):
    placed = (
        P(None, ("groups", "tok"), None),
        P(None, ("groups", "tok"), None),
        P("groups", "tok", None),
        P("groups", "tok", None),
        P("groups", None),
        P(("groups", "tok")),
    )
    return jax.shard_map(
        per_device,
        mesh=mesh,
        in_specs=placed,
        out_specs=P(("groups", "tok"), None),
        check_vma=False,
    )
```

profile of v0, /device:TPU:1, one launch (start us, length us, event | category | flops | bytes accessed | tf_op | source)
XLA Modules:
  0.0 147.8 jit_solution(14041610911955827750)
XLA Ops:
  6.5 0.8 compare_and_fusion.1
  7.3 1.1 fusion.11
  8.4 0.2 copy.15
  8.6 0.2 copy.16
  8.7 1.1 fusion.10
  9.8 0.2 copy.17
  10.0 0.6 gather_fusion
  10.6 0.6 gather_fusion.2
  11.2 0.2 copy.18
  11.3 0.6 gather_fusion.1
  11.9 0.6 gather_fusion.3
  12.5 0.1 broadcast_select_fusion
  12.6 0.8 pad_maximum_fusion.1
  13.4 0.0 all-gather.3.cloned.1.call-start
  13.4 0.7 pad_maximum_fusion
  14.2 0.0 all-gather.3.cloned.1.call-update
  14.9 54.4 %all-gather.5.cloned.1.call-done = bf16[2,2048,512]{1,2,0:T(8,128)(2,1)} async-done(((bf16[2,128,512]{1,2,0:T(8,128)(2,1)}), bf16[2,2048,512]{1,2,0:T(8,128)(2,1)}) %all-gather.5.cloned.1.call-update) | async-done | bytes 4194320 | tf_op jit(solution)/shard_map/all_gather | solution.py:32
  69.3 6.2 %fusion = f32[2,64,8,8]{3,2,1,0:T(8,128)S(1)} fusion(bf16[2,2048,512]{1,2,0:T(8,128)(2,1)} %all-gather.5.cloned.1.call-done), kind=kOutput, calls=%fused_computation.4 | convolution fusion | flops 33554432 | bytes 4227072 | tf_op jit(solution)/shard_map/lkqr,lkqs->lqrs/dot_general | solution.py:21
  75.4 47.4 %all-gather.3.cloned.1.call-done = bf16[2,2048,512]{1,2,0:T(8,128)(2,1)} async-done(((bf16[2,128,512]{1,2,0:T(8,128)(2,1)}), bf16[2,2048,512]{1,2,0:T(8,128)(2,1)}) %all-gather.3.cloned.1.call-update) | async-done | bytes 4194320 | tf_op jit(solution)/shard_map/all_gather | solution.py:31
  122.8 6.6 %fusion.7 = f32[64]{0:T(128)S(1)} fusion(f32[2,64,8,8]{3,2,1,0:T(8,128)S(1)} %fusion, bf16[2,2048,512]{1,2,0:T(8,128)(2,1)} %all-gather.3.cloned.1.call-done), kind=kOutput, calls=%fused_computation.11 | convolution fusion | flops 33570752 | bytes 4227328 | tf_op jit(solution)/shard_map/lkqr,lkqs->lqrs/dot_general | solution.py:21
  129.5 7.0 %fusion.12 = f32[2,512,640]{2,1,0:T(8,128)S(1)} fusion(bf16[2,2048,512]{1,2,0:T(8,128)(2,1)} %all-gather.3.cloned.1.call-done, bf16[2,640,2048]{2,1,0:T(8,128)(2,1)} %param.9), kind=kOutput, calls=%fused_computation.29 | convolution fusion | flops 2684354560 | bytes 12058624 | tf_op jit(solution)/shard_map/ltk,lkc->ltc/dot_general | solution.py:34
  136.5 3.4 %multiply_reduce_fusion = f32[512,640]{1,0:T(8,128)S(1)} fusion(f32[2,512,640]{2,1,0:T(8,128)S(1)} %fusion.12, bf16[2,2048,512]{1,2,0:T(8,128)(2,1)S(1)} %copy-done, bf16[2,640,2048]{2,1,0:T(8,128)(2,1)S(1)} %bitcast.51), kind=kOutput, calls=%fused_computation.8 | convolution fusion | flops 2685337600 | bytes 13369344 | tf_op jit(solution)/shard_map/ltk,lkc->ltc/dot_general | solution.py:35
  139.9 0.3 bitcast_reduce_fusion
  140.3 0.8 divide_select_fusion
  (13 shorter events, 0.1 us)
Async XLA Ops:
  6.5 62.7 %all-gather.5.cloned.1.call-start = ((), (), s32[]{:S(2)}) async-start(), calls=%async_computation.1 | async-start | bytes 4456448 | tf_op jit(solution)/shard_map/all_gather | solution.py:32
  13.4 109.5 %all-gather.3.cloned.1.call-start = ((), (), s32[]{:S(2)}) async-start(), calls=%async_computation | async-start | bytes 4456448 | tf_op jit(solution)/shard_map/all_gather | solution.py:31
  122.8 13.6 %slice-start = ((s8[5242880]{0:T(1024)(128)(4,1)}), s8[4194304]{0:T(1024)(128)(4,1)S(1)}, s32[]{:S(2)}) async-start(s8[5242880]{0:T(1024)(128)(4,1)} %bitcast.50), calls=%async_computation.2 | async-start | bytes 8388608
  129.5 7.0 %slice-start.1 = ((s8[5242880]{0:T(1024)(128)(4,1)}), s8[1048576]{0:T(1024)(128)(4,1)S(1)}, s32[]{:S(2)}) async-start(s8[5242880]{0:T(1024)(128)(4,1)} %bitcast.50), calls=%async_computation.3 | async-start | bytes 2097152
  129.5 7.0 %copy-start = (bf16[2,2048,512]{1,2,0:T(8,128)(2,1)S(1)}, bf16[2,2048,512]{1,2,0:T(8,128)(2,1)}, u32[]{:S(2)}) copy-start(bf16[2,2048,512]{1,2,0:T(8,128)(2,1)} %all-gather.5.cloned.1.call-done) | copy-start | bytes 12582916
Sparse Core Ops, SparseCore 0:
  13.5 55.7 all-gather.4
  71.4 51.3 all-gather.2
where the time goes:
time: 148 us
  waiting for transfers between devices  102 us (69%)
  matrix products  23.2 us (16%)
  between operations  14.2 us (10%)
  local copies, waits for them, and re-layouts  5.13 us (3%)
  other arithmetic  3.46 us (2%)
    all_gather x1, waiting for transfers between devices, per_device(): lax.all_gather(picked_v, 'tok', axis=1, tiled=True)  54.4 us
    all_gather x1, waiting for transfers between devices, per_device(): lax.all_gather(picked_u, 'tok', axis=1, tiled=True)  47.4 us
    dot_general x2, matrix products, rank_grams(): jnp.einsum('lkqr,lkqs->lqrs', per, per, preferred_element_type=jnp.float32)  12.8 us
    dot_general x1, matrix products, per_device(): jnp.einsum('ltk,lkc->ltc', gradients, whole_u, preferred_element_type=jnp...  6.96 us
    dot_general x1, matrix products, per_device(): jnp.einsum('ltk,lkc->ltc', activations, whole_v, preferred_element_type=j...  3.44 us
  transfers between devices with their start and end apart: 2, of which 2 were waited for; matrix products, arithmetic and copies ran while one was open for 5% of the time, Pallas kernels for 0%

commit v1 on v0

v1 whole, which is shorter than its diff:
```python
import functools

import jax
import jax.numpy as jnp
from jax import lax
from jax.experimental import pallas as pl
from jax.experimental.pallas import tpu as pltpu
from jax.sharding import PartitionSpec as P

RANK = 8
QB = 4
WIDTH = QB * RANK
Z = 4
X = 2
CORES = 2
CHIPS = Z * X
HALF = 256
AROUND = 1
MESH = pl.DeviceIdType.MESH


def column_names(block_ids):
    within = jnp.arange(block_ids.shape[1] * WIDTH, dtype=jnp.int32) % WIDTH
    return jnp.repeat(block_ids, WIDTH, axis=1) * WIDTH + within[None, :]


def pick_columns(factor, names):
    rows = jnp.arange(factor.shape[2], dtype=jnp.int32)
    pick = (rows[None, :, None] == names[:, None, :]).astype(factor.dtype)
    chosen = jnp.einsum("lkn,lnc->lkc", factor, pick, preferred_element_type=jnp.float32)
    return chosen.astype(factor.dtype)


def rank_grams(factor):
    per = factor.reshape(factor.shape[0], factor.shape[1], -1, RANK)
    return jnp.einsum("lkqr,lkqs->lqrs", per, per, preferred_element_type=jnp.float32)


def gathered(activations, gradients, query_u, query_v, block_ids):
    layers, tok_rows, _ = activations.shape
    queries = block_ids.shape[1] * QB
    names = column_names(block_ids)
    whole_u = lax.all_gather(pick_columns(query_u, names), "tok", axis=1, tiled=True)
    whole_v = lax.all_gather(pick_columns(query_v, names), "tok", axis=1, tiled=True)
    grad_proj = jnp.einsum("ltk,lkc->ltc", gradients, whole_u, preferred_element_type=jnp.float32)
    act_proj = jnp.einsum("ltk,lkc->ltc", activations, whole_v, preferred_element_type=jnp.float32)
    raw = jnp.sum((grad_proj * act_proj).reshape(layers, tok_rows, queries, RANK), axis=(0, 3))
    norm_sq = jnp.sum(rank_grams(whole_u) * rank_grams(whole_v), axis=(0, 2, 3))
    return raw / jnp.sqrt(norm_sq + 1e-06)[None, :]


def split_dot(value, ones, parts):
    total = None
    for _ in range(parts):
        head = value.astype(jnp.bfloat16)
        term = jnp.dot(head, ones, preferred_element_type=jnp.float32)
        total = term if total is None else total + term
        value = value - head.astype(jnp.float32)
    return total


def kernel(layers, halves, act_ref, grad_ref, qu_ref, qv_ref, col_ref, out_ref,
           whole, toks, acc, gram, tok_sem, send_sem, recv_sem):
    pieces = layers * halves * 2
    shard = qu_ref.shape[1]
    bank = qu_ref.shape[2]
    depth = CORES * shard
    me = lax.axis_index("tok")
    c = lax.rem(me, CORES)
    x = lax.rem(me // CORES, X)
    z = me // (CORES * X)

    def device(zz, xx, cc):
        return (zz * X + xx) * CORES + cc

    targets = (
        device(lax.rem(z + 1, Z), x, c),
        device(lax.rem(z + Z - 1, Z), x, c),
        device(z, 1 - x, c),
        device(z, x, 1 - c),
    )

    loads = []
    for layer in range(layers):
        for side, ref in enumerate((grad_ref, act_ref)):
            m = layer * 2 + side
            loads.append(pltpu.make_async_copy(ref.at[layer], toks.at[m], tok_sem.at[m]))
    for load in loads:
        load.start()

    barrier = pltpu.get_barrier_semaphore()

    def greet(target):
        pl.semaphore_signal(barrier, inc=1, device_id={"tok": target}, device_id_type=MESH)

    @pl.when(z < Z - 1)
    def _():
        greet(targets[0])

    @pl.when(z > 0)
    def _():
        greet(targets[1])

    greet(targets[2])
    greet(targets[3])

    def copy(direction, zz, xx, p):
        chip = zz * X + xx
        rows = pl.ds(pl.multiple_of(device(zz, xx, c) * shard, shard), shard)
        return pltpu.make_async_remote_copy(
            src_ref=whole.at[p, rows],
            dst_ref=whole.at[p, rows],
            send_sem=send_sem.at[direction, chip, p],
            recv_sem=recv_sem.at[1 if direction == 3 else 0, chip, p],
            device_id={"tok": targets[direction]},
            device_id_type=MESH,
        )

    def from_core(zz, xx, p):
        chip = zz * X + xx
        rows = pl.ds(pl.multiple_of(device(zz, xx, 1 - c) * shard, shard), shard)
        return pltpu.make_async_remote_copy(
            src_ref=whole.at[p, rows],
            dst_ref=whole.at[p, rows],
            send_sem=send_sem.at[3, chip, p],
            recv_sem=recv_sem.at[1, chip, p],
            device_id={"tok": targets[3]},
            device_id_type=MESH,
        )

    def routes(zz, xx, p):
        mine = xx == x
        around = p >= pieces - AROUND
        along = jnp.logical_or(mine, around)
        return (
            along & (zz <= z) & (z < Z - 1),
            along & (zz >= z) & (z > 0),
            mine & jnp.logical_or(zz == z, jnp.logical_not(around)),
        )

    def forward(zz, xx, p):
        for direction, wanted in enumerate(routes(zz, xx, p)):
            @pl.when(wanted)
            def _(direction=direction):
                copy(direction, zz, xx, p).start()
        copy(3, zz, xx, p).start()

    own_rows = pl.ds(pl.multiple_of(me * shard, shard), shard)
    entered = False
    for layer in range(layers):
        for h in range(halves):
            wanted = col_ref[pl.ds(layer, 1), pl.ds(h * HALF, HALF)]
            names = lax.broadcasted_iota(jnp.int32, (bank, HALF), 0)
            pick = jnp.where(names == wanted, 1.0, 0.0).astype(jnp.bfloat16)
            for side, ref in enumerate((qu_ref, qv_ref)):
                p = (layer * halves + h) * 2 + side
                whole[p, own_rows] = jnp.dot(
                    ref[layer], pick, preferred_element_type=jnp.float32
                ).astype(jnp.bfloat16)
                if not entered:
                    pl.semaphore_wait(
                        barrier, 2 + jnp.where(z > 0, 1, 0) + jnp.where(z < Z - 1, 1, 0)
                    )
                    entered = True
                forward(z, x, jnp.int32(p))

    def clear(p, carry):
        acc[p] = jnp.zeros(acc.shape[1:], acc.dtype)
        gram[p] = jnp.zeros(gram.shape[1:], gram.dtype)
        return carry

    lax.fori_loop(0, pieces, clear, 0)
    for load in loads:
        load.wait()

    def use(zz, xx, p):
        from_core(zz, xx, p).wait_recv()
        chip = zz * X + xx
        rows = pl.ds(pl.multiple_of(chip * depth, depth), depth)
        m = (p // (2 * halves)) * 2 + lax.rem(p, 2)
        block = whole[p, rows]
        acc[p] += jnp.dot(toks[m, :, rows], block, preferred_element_type=jnp.float32)
        gram[p] += lax.dot_general(
            block, block, (((0,), (0,)), ((), ())), preferred_element_type=jnp.float32
        )

    def events(t):
        j, p = t // pieces, lax.rem(t, pieces)
        near = (j >= 1) & (j < Z)
        k = j - 1
        end = (z == 0) | (z == Z - 1)
        i = (k - 1) * pieces + p
        mixed = jnp.logical_not(end) & (k >= 1) & (k < Z - 1)
        far = jnp.where(z < 2, k, Z - 1 - k)
        beside = jnp.where(lax.rem(i, 2) == 0, z - 1, z + 1)
        source = jnp.where(k == 0, z, jnp.where(mixed, beside, far))
        piece = jnp.where(mixed, i // 2, p)
        return (
            (near & (z - j >= 0), z - j, x, p),
            (near & (z + j <= Z - 1), z + j, x, p),
            ((j >= 1) & (j <= Z), source, 1 - x, piece),
        )

    def step(t, carry):
        for valid, zz, xx, p in events(t):
            @pl.when(valid)
            def _(zz=zz, xx=xx, p=p):
                copy(2, zz, xx, p).wait_recv()
                forward(zz, xx, p)

        @pl.when(t < 2 * pieces)
        def _():
            use(z, x, t - pieces)

        for valid, zz, xx, p in events(t - 1):
            @pl.when(valid)
            def _(zz=zz, xx=xx, p=p):
                use(zz, xx, p)
        return carry

    lax.fori_loop(pieces, (Z + 1) * pieces + 1, step, 0)

    raw = None
    norm = None
    for h in range(halves):
        spot = lax.broadcasted_iota(jnp.int32, (HALF, out_ref.shape[1]), 0) // RANK
        query = lax.broadcasted_iota(jnp.int32, (HALF, out_ref.shape[1]), 1)
        ones = jnp.where(spot + h * (HALF // RANK) == query, 1.0, 0.0).astype(jnp.bfloat16)
        product = None
        grams = None
        for layer in range(layers):
            p = (layer * halves + h) * 2
            term = acc[p] * acc[p + 1]
            both = gram[p] * gram[p + 1]
            product = term if product is None else product + term
            grams = both if grams is None else grams + both
        down = lax.broadcasted_iota(jnp.int32, (HALF, HALF), 0) // RANK
        across = lax.broadcasted_iota(jnp.int32, (HALF, HALF), 1) // RANK
        column = jnp.sum(jnp.where(down == across, grams, 0.0), axis=0, keepdims=True)
        column = jnp.broadcast_to(column, (8, HALF))
        part = split_dot(product, ones, 2)
        squares = split_dot(column, ones, 3)
        raw = part if raw is None else raw + part
        norm = squares if norm is None else norm + squares
    out_ref[...] = raw * (1.0 / jnp.sqrt(norm[0:1] + 1e-06))

    def drain(n, carry):
        chip, p = n // pieces, lax.rem(n, pieces)
        zz, xx = chip // X, lax.rem(chip, X)
        for direction, wanted in enumerate(routes(zz, xx, p)):
            @pl.when(wanted)
            def _(direction=direction):
                copy(direction, zz, xx, p).wait_send()
        copy(3, zz, xx, p).wait_send()
        return carry

    lax.fori_loop(0, CHIPS * pieces, drain, 0)


def passed_on(activations, gradients, query_u, query_v, block_ids):
    layers, tok_rows, width = activations.shape
    columns = block_ids.shape[1] * WIDTH
    halves = columns // HALF
    pieces = layers * halves * 2
    names = column_names(block_ids)
    flops = 2 * 2 * layers * columns * width * (tok_rows + HALF)
    return pl.pallas_call(
        functools.partial(kernel, layers, halves),
        out_shape=jax.ShapeDtypeStruct((tok_rows, columns // RANK), jnp.float32),
        in_specs=[pl.BlockSpec(memory_space=pl.ANY)] * 2
        + [pl.BlockSpec(memory_space=pltpu.VMEM)] * 3,
        out_specs=pl.BlockSpec(memory_space=pltpu.VMEM),
        scratch_shapes=[
            pltpu.VMEM((pieces, width, HALF), jnp.bfloat16),
            pltpu.VMEM((layers * 2, tok_rows, width), jnp.bfloat16),
            pltpu.VMEM((pieces, tok_rows, HALF), jnp.float32),
            pltpu.VMEM((pieces, HALF, HALF), jnp.float32),
            pltpu.SemaphoreType.DMA((layers * 2,)),
            pltpu.SemaphoreType.DMA((4, CHIPS, pieces)),
            pltpu.SemaphoreType.DMA((2, CHIPS, pieces)),
        ],
        compiler_params=pltpu.CompilerParams(
            collective_id=0, has_side_effects=True, vmem_limit_bytes=56 * 1024 * 1024
        ),
        cost_estimate=pl.CostEstimate(
            flops=flops, bytes_accessed=12 * 1024 * 1024, transcendentals=0
        ),
    )(activations, gradients, query_u, query_v, names)


def per_device(on_grid, activations, gradients, query_u, query_v, block_ids, counts):
    arrange = passed_on if on_grid else gathered
    scaled = arrange(activations, gradients, query_u, query_v, block_ids)
    live = jnp.arange(scaled.shape[0], dtype=jnp.int32) < counts[0]
    return jnp.where(live[:, None], scaled, jnp.zeros_like(scaled))


def solution(mesh):
    placed = (
        P(None, ("groups", "tok"), None),
        P(None, ("groups", "tok"), None),
        P("groups", "tok", None),
        P("groups", "tok", None),
        P("groups", None),
        P(("groups", "tok")),
    )
    return jax.shard_map(
        functools.partial(per_device, mesh.shape["tok"] == CHIPS * CORES),
        mesh=mesh,
        in_specs=placed,
        out_specs=P(("groups", "tok"), None),
        check_vma=False,
    )
```

time: 148 us -> 63.5 us (0.43)
  waiting for transfers between devices: 102 us -> 0 us
  Pallas kernels: 0 us -> 59.3 us
  matrix products: 23.2 us -> 0 us
  between operations: 14.2 us -> 0.68 us
  local copies, waits for them, and re-layouts: 5.13 us -> 0.97 us
    all_gather x2 -> x0, waiting for transfers between devices: 102 us -> none  [the longest x1 54.4 us: per_device(): lax.all_gather(picked_v, 'tok', axis=1, tiled=True)]
    pallas_call x0 -> x1, Pallas kernels: none -> 59.3 us  [passed_on(): pl.pallas_call(functools.partial(kernel, layers, halves), out_shape=jax.S...]
    dot_general x4 -> x0, matrix products: 23.2 us -> none  [the longest x2 12.8 us: rank_grams(): jnp.einsum('lkqr,lkqs->lqrs', per, per, preferred_element_type=jnp.float32)]
    gather x4 -> x0, local copies, waits for them, and re-layouts: 2.31 us -> none  [pick_columns(): jnp.take(slots, block_ids[layer], axis=1).reshape(factor.shape[1], -1)]
    slice x2 -> x0, local copies, waits for them, and re-layouts: 2.14 us -> none  [pick_columns(): slots = factor[layer].reshape(factor.shape[1], -1, width)]
    another operation x2 -> x0, other arithmetic: 1.49 us -> none  [pick_columns(): return jnp.stack(chosen)]
  transfers between devices with their start and end apart: 2 -> 0, of which waited for: 2 -> 0; matrix products, arithmetic and copies ran while one was open for 5% -> 0% of each run, Pallas kernels for 0% -> 0%
where the time goes in v1:
time: 63.5 us; the launch traced here: 63.3 us
  Pallas kernels  59.3 us (93%)
  other arithmetic  2.41 us (4%)
  local copies, waits for them, and re-layouts  0.97 us (2%)
  between operations  0.68 us (1%)
    pallas_call x1, Pallas kernels, passed_on(): pl.pallas_call(functools.partial(kernel, layers, halves), out_shape=jax.S...  59.3 us

profile of v1, /device:TPU:1, one launch (start us, length us, event | category | flops | bytes accessed | tf_op | source)
XLA Modules:
  0.0 63.3 jit_solution(15452084333567254178)
XLA Ops:
  0.7 0.7 %broadcast_multiply_fusion = s32[2,16]{1,0:T(2,128)S(1)} fusion(s32[2,16]{1,0:T(2,128)} %param.10), kind=kLoop, calls=%fused_computation.8 | loop fusion | flops 32 | bytes 256 | tf_op jit(solution)/shard_map/mul | solution.py:24
  1.4 0.1 broadcast_in_dim.17
  1.4 0.1 mul.12
  1.5 0.6 broadcast_add_fusion.col_ref
  2.1 59.3 %shard_map.64 = f32[640,64]{1,0:T(8,128)} custom-call(bf16[2,640,2048]{2,1,0:T(8,128)(2,1)} %act_ref.1, bf16[2,640,2048]{2,1,0:T(8,128)(2,1)} %grad_ref.1, bf16[2,128,1024]{2,1,0:T(8,128)(2,1)} %qu_ref.1, bf16[2,128,1024]{2,1,0:T(8,128)(2,1)} %qv_ref.1, s32[2,512]{1,0:T(2,128)} %broadcast_add_fusion.col_ref), custom_call_target="tpu_custom_call" | custom-call | flops 7516192768 | bytes 12582912 | tf_op jit(solution)/shard_map/pallas_call | solution.py:267
  61.4 1.1 %broadcast_select_fusion = f32[640,64]{1,0:T(8,128)S(1)} fusion(f32[640,64]{1,0:T(8,128)} %shard_map.64, pred[640]{0:T(1024)(128)(4,1)S(1)} %iota_compare_fusion), kind=kLoop, calls=%fused_computation | loop fusion | flops 40960 | bytes 328320 | tf_op jit(solution)/shard_map/jit(_where)/select_n | solution.py:295
  62.5 0.8 %copy.7 = f32[640,64]{0,1:T(8,128)} copy(f32[640,64]{1,0:T(8,128)S(1)} %broadcast_select_fusion) | data formatting | bytes 327680 | tf_op jit(solution)/shard_map/jit(_where)/select_n | solution.py:295
  (2 shorter events, 0.0 us)

commit v2 on v1

--- a/solution.py
+++ b/solution.py
@@ -46,14 +46,16 @@
     act_proj = jnp.einsum("ltk,lkc->ltc", activations, whole_v, preferred_element_type=jnp.float32)
     raw = jnp.sum((grad_proj * act_proj).reshape(layers, tok_rows, queries, RANK), axis=(0, 3))
     norm_sq = jnp.sum(rank_grams(whole_u) * rank_grams(whole_v), axis=(0, 2, 3))
-    return raw / jnp.sqrt(norm_sq + 1e-06)[None, :]
+    return (raw / jnp.sqrt(norm_sq + 1e-06)[None, :]).T
 
 
 def split_dot(value, ones, parts):
     total = None
     for _ in range(parts):
         head = value.astype(jnp.bfloat16)
-        term = jnp.dot(head, ones, preferred_element_type=jnp.float32)
+        term = lax.dot_general(
+            ones, head, (((1,), (1,)), ((), ())), preferred_element_type=jnp.float32
+        )
         total = term if total is None else total + term
         value = value - head.astype(jnp.float32)
     return total
@@ -130,7 +132,7 @@
 
     def routes(zz, xx, p):
         mine = xx == x
-        around = p >= pieces - AROUND
+        around = p < AROUND
         along = jnp.logical_or(mine, around)
         return (
             along & (zz <= z) & (z < Z - 1),
@@ -149,7 +151,11 @@
     entered = False
     for layer in range(layers):
         for h in range(halves):
-            wanted = col_ref[pl.ds(layer, 1), pl.ds(h * HALF, HALF)]
+            lane = lax.broadcasted_iota(jnp.int32, (1, HALF), 1)
+            wanted = lane % WIDTH
+            for b in range(HALF // WIDTH):
+                start = col_ref[layer, h * (HALF // WIDTH) + b] * WIDTH
+                wanted = wanted + jnp.where(lane // WIDTH == b, start, 0)
             names = lax.broadcasted_iota(jnp.int32, (bank, HALF), 0)
             pick = jnp.where(names == wanted, 1.0, 0.0).astype(jnp.bfloat16)
             for side, ref in enumerate((qu_ref, qv_ref)):
@@ -223,8 +229,8 @@
     raw = None
     norm = None
     for h in range(halves):
-        spot = lax.broadcasted_iota(jnp.int32, (HALF, out_ref.shape[1]), 0) // RANK
-        query = lax.broadcasted_iota(jnp.int32, (HALF, out_ref.shape[1]), 1)
+        spot = lax.broadcasted_iota(jnp.int32, (out_ref.shape[0], HALF), 1) // RANK
+        query = lax.broadcasted_iota(jnp.int32, (out_ref.shape[0], HALF), 0)
         ones = jnp.where(spot + h * (HALF // RANK) == query, 1.0, 0.0).astype(jnp.bfloat16)
         product = None
         grams = None
@@ -242,7 +248,7 @@
         squares = split_dot(column, ones, 3)
         raw = part if raw is None else raw + part
         norm = squares if norm is None else norm + squares
-    out_ref[...] = raw * (1.0 / jnp.sqrt(norm[0:1] + 1e-06))
+    out_ref[...] = raw * (1.0 / jnp.sqrt(norm[:, 0:1] + 1e-06))
 
     def drain(n, carry):
         chip, p = n // pieces, lax.rem(n, pieces)
@@ -262,13 +268,13 @@
     columns = block_ids.shape[1] * WIDTH
     halves = columns // HALF
     pieces = layers * halves * 2
-    names = column_names(block_ids)
     flops = 2 * 2 * layers * columns * width * (tok_rows + HALF)
     return pl.pallas_call(
         functools.partial(kernel, layers, halves),
-        out_shape=jax.ShapeDtypeStruct((tok_rows, columns // RANK), jnp.float32),
+        out_shape=jax.ShapeDtypeStruct((columns // RANK, tok_rows), jnp.float32),
         in_specs=[pl.BlockSpec(memory_space=pl.ANY)] * 2
-        + [pl.BlockSpec(memory_space=pltpu.VMEM)] * 3,
+        + [pl.BlockSpec(memory_space=pltpu.VMEM)] * 2
+        + [pl.BlockSpec(memory_space=pltpu.SMEM)],
         out_specs=pl.BlockSpec(memory_space=pltpu.VMEM),
         scratch_shapes=[
             pltpu.VMEM((pieces, width, HALF), jnp.bfloat16),
@@ -285,14 +291,14 @@
         cost_estimate=pl.CostEstimate(
             flops=flops, bytes_accessed=12 * 1024 * 1024, transcendentals=0
         ),
-    )(activations, gradients, query_u, query_v, names)
+    )(activations, gradients, query_u, query_v, block_ids)
 
 
 def per_device(on_grid, activations, gradients, query_u, query_v, block_ids, counts):
     arrange = passed_on if on_grid else gathered
     scaled = arrange(activations, gradients, query_u, query_v, block_ids)
-    live = jnp.arange(scaled.shape[0], dtype=jnp.int32) < counts[0]
-    return jnp.where(live[:, None], scaled, jnp.zeros_like(scaled))
+    live = jnp.arange(scaled.shape[1], dtype=jnp.int32) < counts[0]
+    return jnp.where(live[None, :], scaled, jnp.zeros_like(scaled)).T
 
 
 def solution(mesh):

time: 63.5 us -> 59.6 us (0.939)
  Pallas kernels: 59.3 us -> 57.1 us
  local copies, waits for them, and re-layouts: 0.97 us -> 0 us
  other arithmetic: 2.41 us -> 1.6 us
    pallas_call x1, Pallas kernels: 59.3 us -> 57.1 us  [passed_on(): pl.pallas_call(functools.partial(kernel, layers, halves), out_shape=jax.S...]
    transpose x0 -> x1, other arithmetic: none -> 1.6 us  [per_device(): return jnp.where(live[None, :], scaled, jnp.zeros_like(scaled)).T]
    select_n x2 -> x0, other arithmetic: 1.13 us -> none  [the longest x1 1.12 us: per_device(): return jnp.where(live[:, None], scaled, jnp.zeros_like(scaled))]
    select_n x1 -> x0, local copies, waits for them, and re-layouts: 0.82 us -> none  [per_device(): return jnp.where(live[:, None], scaled, jnp.zeros_like(scaled))]
    mul x1 -> x0, other arithmetic: 0.68 us -> none  [column_names(): return jnp.repeat(block_ids, WIDTH, axis=1) * WIDTH + within[None, :]]
where the time goes in v2:
time: 59.6 us; the launch traced here: 59.4 us
  Pallas kernels  57.1 us (96%)
  other arithmetic  1.6 us (3%)
  between operations  0.67 us (1%)
    pallas_call x1, Pallas kernels, passed_on(): pl.pallas_call(functools.partial(kernel, layers, halves), out_shape=jax.S...  57.1 us
    transpose x1, other arithmetic, per_device(): return jnp.where(live[None, :], scaled, jnp.zeros_like(scaled)).T  1.6 us

profile of v2, /device:TPU:1, one launch (start us, length us, event | category | flops | bytes accessed | tf_op | source)
XLA Modules:
  0.0 59.4 jit_solution(2236778406758671268)
XLA Ops:
  0.7 57.1 %shard_map.64 = f32[64,640]{1,0:T(8,128)} custom-call(bf16[2,640,2048]{2,1,0:T(8,128)(2,1)} %act_ref.1, bf16[2,640,2048]{2,1,0:T(8,128)(2,1)} %grad_ref.1, bf16[2,128,1024]{2,1,0:T(8,128)(2,1)} %qu_ref.1, bf16[2,128,1024]{2,1,0:T(8,128)(2,1)} %qv_ref.1, s32[2,16]{1,0:T(2,128)} %col_ref.1), custom_call_target="tpu_custom_call" | custom-call | flops 7516192768 | bytes 12582912 | tf_op jit(solution)/shard_map/pallas_call | solution.py:272
  57.8 1.6 %select_bitcast_fusion = f32[640,64]{0,1:T(8,128)} fusion(f32[64,640]{1,0:T(8,128)} %shard_map.64, pred[640]{0:T(1024)(128)(4,1)S(1)} %iota_compare_fusion), kind=kLoop, calls=%fused_computation | loop fusion | flops 40960 | bytes 328320 | tf_op jit(solution)/shard_map/transpose | solution.py:301
  (1 shorter events, 0.0 us)
